TPU v7x, 32 devices: a whole 2x2x4 slice. The times are simulated.
32 devices in a mesh: layer: 2 (over core), blk: 16 (over z, y, x).
Axes of the slice: x: 2, y: 2, z: 4, core: 2. Of those that a mesh axis runs over, the one named last changes fastest.
Arguments:
- density: float32 [48, 6, 256, 256], P('blk'), may hold values from -0.15625 to 0.15625
- pattern: int32 [48, 6], replicated, may hold values from 0 to 47, as said below
Outputs:
- squared: float32 [48, 6, 256, 256], P('blk', None, None, 'layer')
- purified: float32 [48, 6, 256, 256], P('blk', None, None, 'layer')
Inputs may be any that keep to these rules, and one draw needn't show every extreme that they name: pattern[i, 0] = i and pattern[i, 1 .. 5] = (i + d) mod 48 for 5 distinct nonzero offsets d in -3 .. 3.
All inputs are finite; a program needn't handle non-finite values.
Results may differ from a plain program's by a relative error of at most 0.0016.
Values may be sent and summed in bfloat16 or wider, within the bound.
A program may use at most 64 MiB of HBM per device.

v0:
```python
import jax
import jax.numpy as jnp
from jax import lax
from jax.sharding import PartitionSpec as P

BAND = 3


def padded_2(value, sides, width):
    for axis, dim in sides:
        size, length = (lax.axis_size(axis), value.shape[dim])
        up = [(i, (i + 1) % size) for i in range(size)]
        down = [(j, i) for i, j in up]
        last = lax.slice_in_dim(value, length - width, length, axis=dim)
        initial = lax.slice_in_dim(value, 0, width, axis=dim)
        before = lax.ppermute(last, axis, up)
        after = lax.ppermute(initial, axis, down)
        value = jnp.concatenate([before, value, after], axis=dim)
    return value


def body(density, pattern):
    count_rows, slots, order, _ = density.shape
    width = order // lax.axis_size("layer")
    start_col = lax.axis_index("layer") * width
    total_rows = pattern.shape[0]
    first = lax.axis_index("blk") * count_rows
    own = lax.dynamic_slice_in_dim(pattern, first, count_rows, 0)
    neighbor = pattern[own]
    equal = neighbor[:, :, None, :] == own[:, None, :, None]
    slot = jnp.argmax(equal.astype(jnp.int32), axis=3)
    valid = jnp.any(equal, axis=3).astype(jnp.float32)
    row_ids = first + jnp.arange(count_rows, dtype=jnp.int32)
    offset = (own - row_ids[:, None] + BAND) % total_rows - BAND
    place = jnp.arange(count_rows, dtype=jnp.int32)[:, None] + BAND + offset
    col_part = lax.dynamic_slice_in_dim(density, start_col, width, 3)
    padded = padded_2(col_part, (("blk", 0),), BAND)
    highest = lax.Precision.HIGHEST
    picked = padded[place[:, :, None], slot] * valid[:, :, :, None, None]

    def product(left):
        return jnp.einsum("rsac,rstcb->rtab", left, picked, precision=highest)

    squared = product(density)
    rounded = squared.astype(jnp.bfloat16)
    cubed = product(lax.all_gather(rounded, "layer", axis=3, tiled=True).astype(jnp.float32))
    return (squared, 3.0 * squared - 2.0 * cubed)


def solution(mesh):
    return jax.shard_map(
        body,
        mesh=mesh,
        in_specs=(P("blk", None, None, None), P()),
        out_specs=(P("blk", None, None, "layer"), P("blk", None, None, "layer")),
        check_vma=False,
    )
```

profile of v0, /device:TPU:0, one launch (start us, length us, event | category | flops | bytes accessed | tf_op | source)
XLA Modules:
  0.0 198.7 jit_solution(12994394962820087794)
XLA Ops:
  7.2 0.0 copy-start
  7.2 0.0 all-gather.2.cloned.1.call-start
  7.2 1.8 constant_dynamic-slice_fusion.1
  9.1 7.0 %collective-permute-start.1 = (f32[3,6,256,128]{3,2,1,0:T(8,128)S(1)}, f32[3,6,256,128]{3,2,1,0:T(8,128)}, u32[]{:S(2)}, u32[]{:S(2)}) collective-permute-start(f32[3,6,256,128]{3,2,1,0:T(8,128)S(1)} %constant_dynamic-slice_fusion.1), channel_id=1, source_target_pairs={{1,0},{2,1},{3,2},{4,3},{5,4},{6,5},{7,6},{8,7},{9,8},{10,9},{11,1... | collective-permute-start | bytes 7077896 | tf_op jit(solution)/shard_map/ppermute | solution.py:17
  16.0 0.0 collective-permute-start
  16.0 0.0 copy-done
  16.0 0.1 copy.26
  16.1 0.1 fusion.25
  16.2 0.1 copy.24
  16.3 0.1 copy.29
  16.4 0.1 copy.25
  16.5 0.1 reshape.25
  16.6 0.6 gather_fusion
  17.2 0.5 compare_reduce_fusion
  17.7 0.1 copy.30
  17.8 1.3 fusion.17
  19.1 0.1 fusion.21
  19.2 0.1 reshape.31
  19.3 47.3 %collective-permute-done.1 = f32[3,6,256,128]{3,2,1,0:T(8,128)} collective-permute-done((f32[3,6,256,128]{3,2,1,0:T(8,128)S(1)}, f32[3,6,256,128]{3,2,1,0:T(8,128)}, u32[]{:S(2)}, u32[]{:S(2)}) %collective-permute-start.1) | collective-permute-done | bytes 2359328 | tf_op jit(solution)/shard_map/ppermute | solution.py:17
  66.5 48.4 %collective-permute-done = f32[3,6,256,128]{3,2,1,0:T(8,128)} collective-permute-done((f32[3,6,256,128]{3,2,1,0:T(8,128)S(1)}, f32[3,6,256,128]{3,2,1,0:T(8,128)}, u32[]{:S(2)}, u32[]{:S(2)}) %collective-permute-start) | collective-permute-done | bytes 2359328 | tf_op jit(solution)/shard_map/ppermute | solution.py:16
  115.0 4.8 %pad_maximum_fusion = f32[9,6,256,128]{3,2,1,0:T(8,128)} fusion(f32[3,6,256,128]{3,2,1,0:T(8,128)} %collective-permute-done.1, f32[3,6,256,128]{3,2,1,0:T(8,128)S(1)} %constant_dynamic-slice_fusion.1, f32[3,6,256,128]{3,2,1,0:T(8,128)} %collective-permute-done), kind=kLoop, calls=%fused_computation.6 | loop fusion | flops 3538944 | bytes 14155776 | tf_op jit(solution)/shard_map/concatenate | solution.py:18
  119.7 13.8 %gather_fusion.1 = f32[108,256,128]{2,1,0:T(8,128)} fusion(f32[9,6,256,128]{3,2,1,0:T(8,128)} %pad_maximum_fusion, s32[108]{0:T(128)S(1)} %reshape.31), kind=kCustom, calls=%fused_computation.1 | custom fusion | bytes 28312416 | tf_op jit(solution)/shard_map/gather | solution.py:39
  133.5 15.2 %copy.31 = f32[3,6,6,256,128]{3,4,1,2,0:T(8,128)} copy(f32[3,6,6,256,128]{4,3,2,1,0:T(8,128)} %bitcast.35) | data formatting | bytes 28311552 | tf_op jit(solution)/shard_map/gather | solution.py:39
  148.7 16.8 %fusion.26 = (bf16[3,6,256,128]{2,3,1,0:T(8,128)(2,1)}, f32[3,6,256,128]{2,3,1,0:T(8,128)S(1)}) fusion(f32[3,6,256,256]{3,2,1,0:T(8,128)} %param.2, f32[3,6,6,256,128]{3,4,1,2,0:T(8,128)} %copy.31, f32[3,6,6]{1,2,0:T(8,128)S(1)} %copy.30), kind=kOutput, calls=%fused_computation.35 | convolution fusion | flops 10875764736 | bytes 22413744 | tf_op jit(solution)/shard_map/rsac,rstcb->rtab/dot_general | solution.py:42
  165.4 0.0 all-gather.2.cloned.1.call-update
  165.5 2.0 copy.33
  167.4 9.6 %all-gather.2.cloned.1.call-done = bf16[3,6,256,256]{2,3,1,0:T(8,128)(2,1)} async-done(((bf16[3,6,256,128]{2,3,1,0:T(8,128)(2,1)}), bf16[3,6,256,256]{2,3,1,0:T(8,128)(2,1)}) %all-gather.2.cloned.1.call-update) | async-done | bytes 2359312 | tf_op jit(solution)/shard_map/all_gather | solution.py:46
  177.0 11.8 %bitcast_subtract_fusion = f32[3,6,256,128]{2,3,1,0:T(8,128)} fusion(f32[3,6,256,128]{2,3,1,0:T(8,128)S(1)} %get-tuple-element.13, bf16[3,6,256,256]{2,3,1,0:T(8,128)(2,1)} %all-gather.2.cloned.1.call-done, f32[3,6,6,256,128]{3,4,1,2,0:T(8,128)} %copy.31, f32[3,6,6]{1,2,0:T(8,128)S(1)} %copy.30), kind=kOutput, calls=%fused_computation.11 | convolution fusion | flops 10876944384 | bytes 21234096 | tf_op jit(solution)/shard_map/rsac,rstcb->rtab/dot_general | solution.py:42
  188.8 3.0 %copy.34 = f32[3,6,256,128]{3,2,1,0:T(8,128)} copy(f32[3,6,256,128]{2,3,1,0:T(8,128)} %bitcast_subtract_fusion) | data formatting | bytes 4718592
  (5 shorter events, 0.0 us)
Async XLA Ops:
  7.2 8.9 %copy-start = (s32[48,6]{0,1:T(8,128)S(1)}, s32[48,6]{0,1:T(8,128)}, u32[]{:S(2)}) copy-start(s32[48,6]{0,1:T(8,128)} %param.3) | copy-start | bytes 3460
  7.2 169.9 %all-gather.2.cloned.1.call-start = ((), (), s32[]{:S(2)}) async-start(), calls=%async_computation | async-start | bytes 3538944 | tf_op jit(solution)/shard_map/all_gather | solution.py:46
  9.1 57.5 %collective-permute-start.1 = (f32[3,6,256,128]{3,2,1,0:T(8,128)S(1)}, f32[3,6,256,128]{3,2,1,0:T(8,128)}, u32[]{:S(2)}, u32[]{:S(2)}) collective-permute-start(f32[3,6,256,128]{3,2,1,0:T(8,128)S(1)} %constant_dynamic-slice_fusion.1), channel_id=1, source_target_pairs={{1,0},{2,1},{3,2},{4,3},{5,4},{6,5},{7,6},{8,7},{9,8},{10,9},{11,1... | collective-permute-start | bytes 7077896 | tf_op jit(solution)/shard_map/ppermute | solution.py:17
  16.0 98.9 %collective-permute-start = (f32[3,6,256,128]{3,2,1,0:T(8,128)S(1)}, f32[3,6,256,128]{3,2,1,0:T(8,128)}, u32[]{:S(2)}, u32[]{:S(2)}) collective-permute-start(f32[3,6,256,128]{3,2,1,0:T(8,128)S(1)} %constant_dynamic-slice_fusion.1), channel_id=1, source_target_pairs={{0,1},{1,2},{2,3},{3,4},{4,5},{5,6},{6,7},{7,8},{8,9},{9,10},{10,1... | collective-permute-start | bytes 7077896 | tf_op jit(solution)/shard_map/ppermute | solution.py:16
Sparse Core Ops, SparseCore 0:
  165.6 11.4 all-gather.1
where the time goes:
time: 199 us
  waiting for transfers between devices  105 us (53%)
  local copies, waits for them, and re-layouts  37 us (19%)
  matrix products  28.6 us (14%)
  between operations  14.1 us (7%)
  starting transfers between devices  7.02 us (4%)
  other arithmetic  6.75 us (3%)
    ppermute x1, waiting for transfers between devices, padded_2(): before = lax.ppermute(last, axis, up)  48.4 us
    ppermute x1, waiting for transfers between devices, padded_2(): after = lax.ppermute(initial, axis, down)  47.3 us
    gather x2, local copies, waits for them, and re-layouts, body(): picked = padded[place[:, :, None], slot] * valid[:, :, :, None, None]  28.9 us
    dot_general x2, matrix products, product(): return jnp.einsum('rsac,rstcb->rtab', left, picked, precision=highest)  28.6 us
    all_gather x1, waiting for transfers between devices, body(): lax.all_gather(rounded, 'layer', axis=3, tiled=True).astype(jnp.float32)  9.62 us
    ppermute x1, starting transfers between devices, padded_2(): after = lax.ppermute(initial, axis, down)  6.98 us
    unnamed x5, local copies, waits for them, and re-layouts  5.09 us
    concatenate x1, other arithmetic, padded_2(): value = jnp.concatenate([before, value, after], axis=dim)  4.76 us
  transfers between devices with their start and end apart: 3, of which 3 were waited for; matrix products, arithmetic and copies ran while one was open for 3% of the time, Pallas kernels for 0%

commit v1 on v0

--- a/solution.py
+++ b/solution.py
@@ -1,9 +1,13 @@
 import jax
 import jax.numpy as jnp
 from jax import lax
+from jax.experimental import pallas as pl
+from jax.experimental.pallas import tpu as pltpu
 from jax.sharding import PartitionSpec as P
 
 BAND = 3
+SPAN = 2 * BAND + 1
+MESH = pl.DeviceIdType.MESH
 
 
 def padded_2(value, sides, width):
@@ -47,9 +51,352 @@
     return (squared, 3.0 * squared - 2.0 * cubed)
 
 
+def offsets_of(pattern_ref, row, total, slots):
+    offs = []
+    for u in range(slots):
+        v = pattern_ref[row, u] - row
+        v = jnp.where(v > BAND, v - total, v)
+        v = jnp.where(v < -BAND, v + total, v)
+        offs.append(v)
+    return offs
+
+
+def lacking(offs):
+    s = offs[0]
+    for v in offs[1:]:
+        s = s + v
+    return -s
+
+
+def slot_of(offs, o):
+    u = jnp.int32(0)
+    for v in range(1, len(offs)):
+        u = jnp.where(offs[v] == o, jnp.int32(v), u)
+    return u
+
+
+def step_kernel(pattern_ref, d_ref, sq_hbm, pu_hbm, own, xin, yin, zin, lhi, llo, phi, plo, acc, cub, sl,
+                xs, xr, ys, yr, zs, zr, ss, sr, qs, us):
+    rows, slots, order, _ = d_ref.shape
+    total = pattern_ref.shape[0]
+    half = order // 2
+    layer = lax.axis_index("layer")
+    b = lax.axis_index("blk")
+    nb = lax.axis_size("blk")
+    p = lax.rem(b, 4)
+    x = lax.rem(p, 2)
+    xb = b + 1 - 2 * x
+    y = p // 2
+    yb = b + 2 - 4 * y
+    zup = lax.rem(b + 4, nb)
+    zdn = lax.rem(b + nb - 4, nb)
+    outer = (p == 0) | (p == 3)
+    zt = jnp.where(p == 0, zup, zdn)
+    first = b * rows
+    bf = jnp.bfloat16
+    f32 = jnp.float32
+
+    barrier = pltpu.get_barrier_semaphore()
+    for dev in ((layer, xb), (layer, yb), (layer, zup), (layer, zdn), (1 - layer, b)):
+        pl.semaphore_signal(barrier, inc=1, device_id=dev, device_id_type=MESH)
+
+    su = x
+    ru = 1 - x
+
+    def own_row(n):
+        return jnp.where(su == 1, 2 - n, n)
+
+    def x_copy(n, q):
+        return (own.at[n, q], xin.at[n, q])
+
+    relay = [(n, j) for n in range(3) for j in range(6 - n)]
+    rest = [(1, 0), (2, 0), (2, 1)]
+
+    def relay_place(flag, n, j):
+        return jnp.where(flag == 1, n + j, j)
+
+    def rest_place(flag, n, l):
+        return jnp.where(flag == 1, l, 6 - n + l)
+
+    def xsend(k):
+        if k < 15:
+            n, j = relay[k]
+            q = relay_place(su, n, j)
+        else:
+            n, l = rest[k - 15]
+            q = rest_place(su, n, l)
+        return pltpu.make_async_remote_copy(
+            src_ref=own.at[n, q], dst_ref=xin.at[n, q], send_sem=xs.at[k], recv_sem=xr.at[k],
+            device_id=(layer, xb), device_id_type=MESH), n, q
+
+    def xrecv(k):
+        if k < 15:
+            n, j = relay[k]
+            q = relay_place(ru, n, j)
+        else:
+            n, l = rest[k - 15]
+            q = rest_place(ru, n, l)
+        return pltpu.make_async_remote_copy(
+            src_ref=own.at[n, q], dst_ref=xin.at[n, q], send_sem=xs.at[k], recv_sem=xr.at[k],
+            device_id=(layer, xb), device_id_type=MESH)
+
+    def ycopy(k):
+        n, j = relay[k]
+        return pltpu.make_async_remote_copy(
+            src_ref=xin.at[n, relay_place(ru, n, j)], dst_ref=yin.at[n, j], send_sem=ys.at[k], recv_sem=yr.at[k],
+            device_id=(layer, yb), device_id_type=MESH)
+
+    def zcopy(k):
+        n, j = relay[k]
+        return pltpu.make_async_remote_copy(
+            src_ref=yin.at[n, j], dst_ref=zin.at[n, j], send_sem=zs.at[k], recv_sem=zr.at[k],
+            device_id=(layer, zt), device_id_type=MESH)
+
+    col = pl.multiple_of(layer * half, half)
+    row_offs = [offsets_of(pattern_ref, first + m, total, slots) for m in range(rows)]
+    row_lack = [lacking(o) for o in row_offs]
+
+    sends = []
+    for k in range(18):
+        cp, n, q = xsend(k)
+        m = own_row(n)
+        offs = [jnp.where(su == 1, row_offs[2 - n][u], row_offs[n][u]) for u in range(slots)]
+        lack = jnp.where(su == 1, row_lack[2 - n], row_lack[n])
+        o = q - BAND
+        o = jnp.where(o >= lack, o + 1, o)
+        own[n, q] = d_ref[m, slot_of(offs, o), :, pl.ds(col, half)].astype(bf)
+        if k == 0:
+            pl.semaphore_wait(barrier, 5)
+        cp.start()
+        sends.append(cp)
+
+    state = {"y": 0, "z": 0}
+
+    def pump():
+        k = state["y"]
+        if k < 18:
+            xrecv(k).wait_recv()
+            if k < 15:
+                ycopy(k).start()
+            state["y"] = k + 1
+        z = k - 1
+        if 0 <= z < 15:
+            ycopy(z).wait_recv()
+
+            @pl.when(outer)
+            def _():
+                zcopy(z).start()
+
+    def lay(m, q):
+        offs = row_offs[m]
+        here = (row_lack[m] != q - BAND).astype(f32)
+        u = slot_of(offs, q - BAND)
+        v = d_ref[m, u] * here
+        hi = v.astype(bf)
+        lhi[m, q] = hi
+        llo[m, q] = (v - hi.astype(f32)).astype(bf)
+        w = d_ref[m, u, :, pl.ds(col, half)] * here
+        whi = w.astype(bf)
+        phi[3 + m, q] = whi
+        plo[m, q] = (w - whi.astype(f32)).astype(bf)
+
+    for m in range(rows):
+        for q in range(SPAN):
+            lay(m, q)
+        pump()
+
+    def right(ref, k, d):
+        lo, hi = max(0, -d), min(SPAN, SPAN - d)
+        return jnp.concatenate([ref[k, q] for q in range(lo, hi)], axis=1), lo + d
+
+    def add(target, i, value, e0):
+        for c in range(value.shape[1] // half):
+            target[i, e0 + c] += value[:, c * half:(c + 1) * half]
+
+    def dot(a, c):
+        return jnp.dot(a, c, preferred_element_type=f32)
+
+    acc[...] = jnp.zeros_like(acc)
+    cub[...] = jnp.zeros_like(cub)
+
+    def local_square(i, m):
+        d = m - i
+        hi, e0 = right(phi, 3 + m, d)
+        lo, _ = right(plo, m, d)
+        a, a2 = lhi[i, d + BAND], llo[i, d + BAND]
+        add(acc, i, dot(a, hi) + (dot(a2, hi) + dot(a, lo)), e0)
+
+    def far_square(i, k):
+        d = k - 3 - i
+        hi, e0 = right(phi, k, d)
+        add(acc, i, dot(lhi[i, d + BAND], hi) + dot(llo[i, d + BAND], hi), e0)
+
+    for i in range(rows):
+        for m in range(rows):
+            local_square(i, m)
+            pump()
+
+    while state["y"] < 18:
+        pump()
+
+    def spread(side_up, get, n, m):
+        k = (6 if side_up else 0) + m
+        row = lax.rem(first + (rows if side_up else total - rows) + m, total)
+        lack = lacking(offsets_of(pattern_ref, row, total, slots))
+        lo, hi = (0, 6 - m) if side_up else (3 - m, SPAN)
+        for q in range(lo, hi):
+            o = q - BAND
+            if q == 0:
+                phi[k, q] = (get(n, 0).astype(f32) * (lack != o).astype(f32)).astype(bf)
+                continue
+            prev = get(n, q - 1).astype(f32) * (lack < o).astype(f32)
+            if q < 6:
+                prev = prev + get(n, q).astype(f32) * (lack > o).astype(f32)
+            phi[k, q] = prev.astype(bf)
+
+    @pl.when(x == 0)
+    def _():
+        for n in range(3):
+            spread(True, lambda n, q: xin[n, q], n, 2 - n)
+
+    @pl.when(x == 1)
+    def _():
+        for n in range(3):
+            spread(False, lambda n, q: xin[n, q], n, n)
+
+    @pl.when(outer)
+    def _():
+        for k in range(15):
+            zcopy(k).wait_recv()
+
+    for is_outer, ref in ((True, zin), (False, yin)):
+        cond = outer if is_outer else jnp.logical_not(outer)
+
+        @pl.when(cond & (x == 0))
+        def _(ref=ref):
+            for n in range(3):
+                spread(False, lambda n, q: ref[n, q - n], n, 2 - n)
+
+        @pl.when(cond & (x == 1))
+        def _(ref=ref):
+            for n in range(3):
+                spread(True, lambda n, q: ref[n, q], n, n)
+
+    scopies = []
+    qcopies = []
+    for i in range(rows):
+        for k in list(range(i, 3)) + list(range(6, 7 + i)):
+            far_square(i, k)
+        for q in range(SPAN):
+            here = (row_lack[i] != q - BAND).astype(f32)
+            sl[layer, i, q] = (acc[i, q] * here).astype(bf)
+        cp = pltpu.make_async_remote_copy(
+            src_ref=sl.at[layer, i], dst_ref=sl.at[layer, i], send_sem=ss.at[i], recv_sem=sr.at[i],
+            device_id=(1 - layer, b), device_id_type=MESH)
+        cp.start()
+        scopies.append(cp)
+        cp = pltpu.make_async_copy(acc.at[i], sq_hbm.at[i], qs.at[i])
+        cp.start()
+        qcopies.append(cp)
+
+    ucopies = []
+    for i in range(rows):
+        scopies[i].wait_send()
+        pltpu.make_async_remote_copy(
+            src_ref=sl.at[1 - layer, i], dst_ref=sl.at[1 - layer, i], send_sem=ss.at[i], recv_sem=sr.at[i],
+            device_id=(1 - layer, b), device_id_type=MESH).wait_recv()
+        for k in range(i, i + SPAN):
+            d = k - 3 - i
+            a = jnp.concatenate([sl[0, i, d + BAND], sl[1, i, d + BAND]], axis=1)
+            hi, e0 = right(phi, k, d)
+            v = dot(a, hi)
+            if 3 <= k < 6:
+                lo, _ = right(plo, k - 3, d)
+                v = v + dot(a, lo)
+            add(cub, i, v, e0)
+        for q in range(SPAN):
+            cub[i, q] = 3.0 * acc[i, q] - 2.0 * cub[i, q]
+        cp = pltpu.make_async_copy(cub.at[i], pu_hbm.at[i], us.at[i])
+        cp.start()
+        ucopies.append(cp)
+
+    for cp in sends:
+        cp.wait_send()
+    for k in range(15):
+        ycopy(k).wait_send()
+
+    @pl.when(outer)
+    def _():
+        for k in range(15):
+            zcopy(k).wait_send()
+
+    for cp in qcopies + ucopies:
+        cp.wait()
+
+
+def place_kernel(pattern_ref, sq, pu, sq_out, pu_out, sem):
+    rows, slots = sq_out.shape[:2]
+    total = pattern_ref.shape[0]
+    first = lax.axis_index("blk") * rows
+    copies = []
+    for i in range(rows):
+        offs = offsets_of(pattern_ref, first + i, total, slots)
+        for t in range(slots):
+            e = jnp.clip(offs[t] + BAND, 0, SPAN - 1)
+            for a, (src, dst) in enumerate(((sq, sq_out), (pu, pu_out))):
+                cp = pltpu.make_async_copy(src.at[i, e], dst.at[i, t], sem.at[a, i, t])
+                cp.start()
+                copies.append(cp)
+    for cp in copies:
+        cp.wait()
+
+
+def fused(density, pattern):
+    rows, slots, order, _ = density.shape
+    half = order // 2
+    dense = jax.ShapeDtypeStruct((rows, SPAN, order, half), jnp.float32)
+    vmem, smem, anyspace = (pl.BlockSpec(memory_space=m) for m in (pltpu.VMEM, pltpu.SMEM, pl.ANY))
+    bf, f32 = jnp.bfloat16, jnp.float32
+    dma = pltpu.SemaphoreType.DMA
+    block = (order, half)
+    sq, pu = pl.pallas_call(
+        step_kernel,
+        out_shape=[dense, dense],
+        in_specs=[smem, vmem],
+        out_specs=[anyspace, anyspace],
+        scratch_shapes=[
+            pltpu.VMEM((3, 6) + block, bf),
+            pltpu.VMEM((3, 6) + block, bf),
+            pltpu.VMEM((3, 6) + block, bf),
+            pltpu.VMEM((3, 6) + block, bf),
+            pltpu.VMEM((rows, SPAN, order, order), bf),
+            pltpu.VMEM((rows, SPAN, order, order), bf),
+            pltpu.VMEM((9, SPAN) + block, bf),
+            pltpu.VMEM((rows, SPAN) + block, bf),
+            pltpu.VMEM((rows, SPAN) + block, f32),
+            pltpu.VMEM((rows, SPAN) + block, f32),
+            pltpu.VMEM((2, rows, SPAN) + block, bf),
+            dma((18,)), dma((18,)), dma((15,)), dma((15,)), dma((15,)), dma((15,)),
+            dma((3,)), dma((3,)), dma((3,)), dma((3,)),
+        ],
+        compiler_params=pltpu.CompilerParams(
+            collective_id=0, has_side_effects=True, vmem_limit_bytes=56 * 1024 * 1024),
+        cost_estimate=pl.CostEstimate(flops=10**10, bytes_accessed=10**7, transcendentals=0),
+    )(pattern, density)
+    out = jax.ShapeDtypeStruct((rows, slots, order, half), f32)
+    return pl.pallas_call(
+        place_kernel,
+        out_shape=[out, out],
+        in_specs=[smem, anyspace, anyspace],
+        out_specs=[anyspace, anyspace],
+        scratch_shapes=[dma((2, rows, slots))],
+    )(pattern, sq, pu)
+
+
 def solution(mesh):
+    planes = mesh.shape["layer"] == 2 and mesh.shape["blk"] == 16
     return jax.shard_map(
-        body,
+        fused if planes else body,
         mesh=mesh,
         in_specs=(P("blk", None, None, None), P()),
         out_specs=(P("blk", None, None, "layer"), P("blk", None, None, "layer")),

time: 199 us -> 202 us (1.015)
  Pallas kernels: 0 us -> 200 us
  waiting for transfers between devices: 105 us -> 0 us
  local copies, waits for them, and re-layouts: 37 us -> 1.37 us
  matrix products: 28.6 us -> 0 us
  between operations: 14.1 us -> 0.8 us
  starting transfers between devices: 7.02 us -> 0 us
  other arithmetic: 6.75 us -> 0 us
    pallas_call x0 -> x2, Pallas kernels: none -> 200 us  [the longest x1 145 us: fused(): pl.pallas_call(place_kernel, out_shape=[out, out], in_specs=[smem, anyspa...]
    ppermute x2 -> x0, waiting for transfers between devices: 95.7 us -> none  [the longest x1 48.4 us: padded_2(): before = lax.ppermute(last, axis, up)]
    gather x4 -> x0, local copies, waits for them, and re-layouts: 29.5 us -> none  [the longest x2 28.9 us: body(): picked = padded[place[:, :, None], slot] * valid[:, :, :, None, None]]
    dot_general x2 -> x0, matrix products: 28.6 us -> none  [product(): return jnp.einsum('rsac,rstcb->rtab', left, picked, precision=highest)]
    all_gather x1 -> x0, waiting for transfers between devices: 9.62 us -> none  [body(): lax.all_gather(rounded, 'layer', axis=3, tiled=True).astype(jnp.float32)]
    ppermute x2 -> x0, starting transfers between devices: 6.99 us -> none  [the longest x1 6.98 us: padded_2(): after = lax.ppermute(initial, axis, down)]
    concatenate x3 -> x0, other arithmetic: 4.93 us -> none  [the longest x1 4.76 us: padded_2(): value = jnp.concatenate([before, value, after], axis=dim)]
    unnamed x5 -> x1, local copies, waits for them, and re-layouts: 5.09 us -> 1.37 us
  transfers between devices with their start and end apart: 3 -> 0, of which waited for: 3 -> 0; matrix products, arithmetic and copies ran while one was open for 3% -> 0% of each run, Pallas kernels for 0% -> 0%
where the time goes in v1:
time: 202 us
  Pallas kernels  200 us (99%)
    pallas_call x1, Pallas kernels, fused(): pl.pallas_call(place_kernel, out_shape=[out, out], in_specs=[smem, anyspa...  145 us
    pallas_call x1, Pallas kernels, fused(): pl.pallas_call(step_kernel, out_shape=[dense, dense], in_specs=[smem, vme...  54.5 us

profile of v1, /device:TPU:0, one launch (start us, length us, event | category | flops | bytes accessed | tf_op | source)
XLA Modules:
  0.0 202.1 jit_solution(16285044625782519517)
XLA Ops:
  0.6 1.4 copy.5.pattern_ref
  2.0 54.5 %shard_map.41 = (f32[3,7,256,128]{3,2,1,0:T(8,128)}, f32[3,7,256,128]{3,2,1,0:T(8,128)}) custom-call(s32[48,6]{1,0:T(8,128)} %copy.5.pattern_ref, f32[3,6,256,256]{3,2,1,0:T(8,128)} %d_ref.1), custom_call_target="tpu_custom_call" | custom-call | flops 10000000000 | bytes 10000000 | tf_op jit(solution)/shard_map/pallas_call | solution.py:362
  56.5 145.4 %shard_map.42 = (f32[3,6,256,128]{3,2,1,0:T(8,128)}, f32[3,6,256,128]{3,2,1,0:T(8,128)}) custom-call(s32[48,6]{1,0:T(8,128)} %copy.5.pattern_ref, f32[3,7,256,128]{3,2,1,0:T(8,128)} %get-tuple-element.4.sq, f32[3,7,256,128]{3,2,1,0:T(8,128)} %get-tuple-element.5.pu), custom_call_target="tpu_custom_call" | custom-call | tf_op jit(solution)/shard_map/pallas_call | solution.py:387

commit v2 on v1

--- a/solution.py
+++ b/solution.py
@@ -75,8 +75,8 @@
     return u
 
 
-def step_kernel(pattern_ref, d_ref, sq_hbm, pu_hbm, own, xin, yin, zin, lhi, llo, phi, plo, acc, cub, sl,
-                xs, xr, ys, yr, zs, zr, ss, sr, qs, us):
+def step_kernel(pattern_ref, d_ref, acc, cub, own, xin, yin, zin, lhi, llo, phi, plo, sl,
+                xs, xr, ys, yr, zs, zr, ss, sr):
     rows, slots, order, _ = d_ref.shape
     total = pattern_ref.shape[0]
     half = order // 2
@@ -283,7 +283,6 @@
                 spread(True, lambda n, q: ref[n, q], n, n)
 
     scopies = []
-    qcopies = []
     for i in range(rows):
         for k in list(range(i, 3)) + list(range(6, 7 + i)):
             far_square(i, k)
@@ -295,11 +294,7 @@
             device_id=(1 - layer, b), device_id_type=MESH)
         cp.start()
         scopies.append(cp)
-        cp = pltpu.make_async_copy(acc.at[i], sq_hbm.at[i], qs.at[i])
-        cp.start()
-        qcopies.append(cp)
-
-    ucopies = []
+
     for i in range(rows):
         scopies[i].wait_send()
         pltpu.make_async_remote_copy(
@@ -316,9 +311,6 @@
             add(cub, i, v, e0)
         for q in range(SPAN):
             cub[i, q] = 3.0 * acc[i, q] - 2.0 * cub[i, q]
-        cp = pltpu.make_async_copy(cub.at[i], pu_hbm.at[i], us.at[i])
-        cp.start()
-        ucopies.append(cp)
 
     for cp in sends:
         cp.wait_send()
@@ -329,9 +321,6 @@
     def _():
         for k in range(15):
             zcopy(k).wait_send()
-
-    for cp in qcopies + ucopies:
-        cp.wait()
 
 
 def place_kernel(pattern_ref, sq, pu, sq_out, pu_out, sem):
@@ -354,7 +343,7 @@
 def fused(density, pattern):
     rows, slots, order, _ = density.shape
     half = order // 2
-    dense = jax.ShapeDtypeStruct((rows, SPAN, order, half), jnp.float32)
+    dense = pltpu.VMEM((rows, SPAN, order, half), jnp.float32)
     vmem, smem, anyspace = (pl.BlockSpec(memory_space=m) for m in (pltpu.VMEM, pltpu.SMEM, pl.ANY))
     bf, f32 = jnp.bfloat16, jnp.float32
     dma = pltpu.SemaphoreType.DMA
@@ -363,7 +352,7 @@
         step_kernel,
         out_shape=[dense, dense],
         in_specs=[smem, vmem],
-        out_specs=[anyspace, anyspace],
+        out_specs=[vmem, vmem],
         scratch_shapes=[
             pltpu.VMEM((3, 6) + block, bf),
             pltpu.VMEM((3, 6) + block, bf),
@@ -373,21 +362,19 @@
             pltpu.VMEM((rows, SPAN, order, order), bf),
             pltpu.VMEM((9, SPAN) + block, bf),
             pltpu.VMEM((rows, SPAN) + block, bf),
-            pltpu.VMEM((rows, SPAN) + block, f32),
-            pltpu.VMEM((rows, SPAN) + block, f32),
             pltpu.VMEM((2, rows, SPAN) + block, bf),
             dma((18,)), dma((18,)), dma((15,)), dma((15,)), dma((15,)), dma((15,)),
-            dma((3,)), dma((3,)), dma((3,)), dma((3,)),
+            dma((3,)), dma((3,)),
         ],
         compiler_params=pltpu.CompilerParams(
-            collective_id=0, has_side_effects=True, vmem_limit_bytes=56 * 1024 * 1024),
+            collective_id=0, has_side_effects=True, vmem_limit_bytes=40 * 1024 * 1024),
         cost_estimate=pl.CostEstimate(flops=10**10, bytes_accessed=10**7, transcendentals=0),
     )(pattern, density)
     out = jax.ShapeDtypeStruct((rows, slots, order, half), f32)
     return pl.pallas_call(
         place_kernel,
         out_shape=[out, out],
-        in_specs=[smem, anyspace, anyspace],
+        in_specs=[smem, vmem, vmem],
         out_specs=[anyspace, anyspace],
         scratch_shapes=[dma((2, rows, slots))],
     )(pattern, sq, pu)

time: 202 us -> 64.7 us (0.32)
  Pallas kernels: 200 us -> 57.5 us
  local copies, waits for them, and re-layouts: 1.37 us -> 6.23 us
    pallas_call x1, Pallas kernels: 145 us -> 5.09 us  [fused(): pl.pallas_call(place_kernel, out_shape=[out, out], in_specs=[smem, vmem,...]
    unnamed x1 -> x9, local copies, waits for them, and re-layouts: 1.37 us -> 6.23 us
    pallas_call x1, Pallas kernels: 54.5 us -> 52.4 us  [fused(): pl.pallas_call(step_kernel, out_shape=[dense, dense], in_specs=[smem, vme...]
where the time goes in v2:
time: 64.7 us; the launch traced here: 64.5 us
  Pallas kernels  57.5 us (89%)
  local copies, waits for them, and re-layouts  6.23 us (10%)
  between operations  0.82 us (1%)
    pallas_call x1, Pallas kernels, fused(): pl.pallas_call(step_kernel, out_shape=[dense, dense], in_specs=[smem, vme...  52.4 us
    unnamed x9, local copies, waits for them, and re-layouts  6.23 us
    pallas_call x1, Pallas kernels, fused(): pl.pallas_call(place_kernel, out_shape=[out, out], in_specs=[smem, vmem,...  5.09 us

profile of v2, /device:TPU:0, one launch (start us, length us, event | category | flops | bytes accessed | tf_op | source)
XLA Modules:
  0.0 64.5 jit_solution(10904833330880768386)
XLA Ops:
  0.6 0.8 %copy.5.pattern_ref = s32[48,6]{1,0:T(8,128)S(1)} copy(s32[48,6]{0,1:T(8,128)} %param.3) | data formatting | bytes 2304 | tf_op args[1]
  1.4 0.0 copy-start.3
  1.4 2.3 %copy-done.3 = f32[3,6,256,256]{3,2,1,0:T(8,128)S(1)} copy-done((f32[3,6,256,256]{3,2,1,0:T(8,128)S(1)}, f32[3,6,256,256]{3,2,1,0:T(8,128)}, u32[]{:S(2)}) %copy-start.3) | copy-done | bytes 4718616
  3.7 0.0 copy-start.2
  3.7 52.4 %shard_map.41 = (f32[3,7,256,128]{3,2,1,0:T(8,128)S(1)}, f32[3,7,256,128]{3,2,1,0:T(8,128)S(1)}) custom-call(s32[48,6]{1,0:T(8,128)S(1)} %copy.5.pattern_ref, f32[3,6,256,256]{3,2,1,0:T(8,128)S(1)} %copy-done.3), custom_call_target="tpu_custom_call" | custom-call | flops 10000000000 | bytes 10000000 | tf_op jit(solution)/shard_map/pallas_call | solution.py:351
  56.1 0.0 copy-done.2
  56.2 0.0 copy-start
  56.2 1.5 %copy-done = f32[3,7,256,128]{3,2,1,0:T(8,128)} copy-done((f32[3,7,256,128]{3,2,1,0:T(8,128)}, f32[3,7,256,128]{3,2,1,0:T(8,128)S(1)}, u32[]{:S(2)}) %copy-start) | copy-done | bytes 2752536
  57.7 0.0 copy-start.1
  57.7 1.6 %copy-done.1 = f32[3,7,256,128]{3,2,1,0:T(8,128)} copy-done((f32[3,7,256,128]{3,2,1,0:T(8,128)}, f32[3,7,256,128]{3,2,1,0:T(8,128)S(1)}, u32[]{:S(2)}) %copy-start.1) | copy-done | bytes 2752536
  59.3 5.1 %shard_map.42 = (f32[3,6,256,128]{3,2,1,0:T(8,128)}, f32[3,6,256,128]{3,2,1,0:T(8,128)}) custom-call(s32[48,6]{1,0:T(8,128)} %copy-done.2, f32[3,7,256,128]{3,2,1,0:T(8,128)} %copy-done, f32[3,7,256,128]{3,2,1,0:T(8,128)} %copy-done.1), custom_call_target="tpu_custom_call" | custom-call | tf_op jit(solution)/shard_map/pallas_call | solution.py:374
Async XLA Ops:
  1.4 2.3 %copy-start.3 = (f32[3,6,256,256]{3,2,1,0:T(8,128)S(1)}, f32[3,6,256,256]{3,2,1,0:T(8,128)}, u32[]{:S(2)}) copy-start(f32[3,6,256,256]{3,2,1,0:T(8,128)} %d_ref.1) | copy-start | bytes 14155780
  3.7 52.4 %copy-start.2 = (s32[48,6]{1,0:T(8,128)}, s32[48,6]{1,0:T(8,128)S(1)}, u32[]{:S(2)}) copy-start(s32[48,6]{1,0:T(8,128)S(1)} %copy.5.pattern_ref) | copy-start | bytes 3460
  56.2 1.6 %copy-start = (f32[3,7,256,128]{3,2,1,0:T(8,128)}, f32[3,7,256,128]{3,2,1,0:T(8,128)S(1)}, u32[]{:S(2)}) copy-start(f32[3,7,256,128]{3,2,1,0:T(8,128)S(1)} %get-tuple-element.4.sq) | copy-start | bytes 8257540
  57.7 1.6 %copy-start.1 = (f32[3,7,256,128]{3,2,1,0:T(8,128)}, f32[3,7,256,128]{3,2,1,0:T(8,128)S(1)}, u32[]{:S(2)}) copy-start(f32[3,7,256,128]{3,2,1,0:T(8,128)S(1)} %get-tuple-element.5.pu) | copy-start | bytes 8257540

commit v3 on v2

--- a/solution.py
+++ b/solution.py
@@ -75,9 +75,9 @@
     return u
 
 
-def step_kernel(pattern_ref, d_ref, acc, cub, own, xin, yin, zin, lhi, llo, phi, plo, sl,
-                xs, xr, ys, yr, zs, zr, ss, sr):
-    rows, slots, order, _ = d_ref.shape
+def step_kernel(pattern_ref, d_hbm, acc, cub, d0, d1, d2, own, xin, yin, zin, lhi, llo, phi, plo, sl,
+                xs, xr, ys, yr, zs, zr, ss, sr, ds):
+    rows, slots, order, _ = d_hbm.shape
     total = pattern_ref.shape[0]
     half = order // 2
     layer = lax.axis_index("layer")
@@ -106,8 +106,10 @@
     def own_row(n):
         return jnp.where(su == 1, 2 - n, n)
 
-    def x_copy(n, q):
-        return (own.at[n, q], xin.at[n, q])
+    held = (d0, d1, d2)
+    loads = [pltpu.make_async_copy(d_hbm.at[own_row(n)], held[n], ds.at[n]) for n in range(3)]
+    for cp in loads:
+        cp.start()
 
     relay = [(n, j) for n in range(3) for j in range(6 - n)]
     rest = [(1, 0), (2, 0), (2, 1)]
@@ -157,14 +159,18 @@
     row_lack = [lacking(o) for o in row_offs]
 
     sends = []
+    by_n = []
+    for n in range(3):
+        offs = [jnp.where(su == 1, row_offs[2 - n][u], row_offs[n][u]) for u in range(slots)]
+        by_n.append((offs, jnp.where(su == 1, row_lack[2 - n], row_lack[n])))
     for k in range(18):
         cp, n, q = xsend(k)
-        m = own_row(n)
-        offs = [jnp.where(su == 1, row_offs[2 - n][u], row_offs[n][u]) for u in range(slots)]
-        lack = jnp.where(su == 1, row_lack[2 - n], row_lack[n])
+        offs, lack = by_n[n]
+        if k in (0, 6, 11):
+            loads[n].wait()
         o = q - BAND
         o = jnp.where(o >= lack, o + 1, o)
-        own[n, q] = d_ref[m, slot_of(offs, o), :, pl.ds(col, half)].astype(bf)
+        own[n, q] = held[n][slot_of(offs, o), :, pl.ds(col, half)].astype(bf)
         if k == 0:
             pl.semaphore_wait(barrier, 5)
         cp.start()
@@ -187,23 +193,25 @@
             def _():
                 zcopy(z).start()
 
-    def lay(m, q):
-        offs = row_offs[m]
-        here = (row_lack[m] != q - BAND).astype(f32)
+    def lay(n, q):
+        offs, lack = by_n[n]
+        m = own_row(n)
+        here = (lack != q - BAND).astype(f32)
         u = slot_of(offs, q - BAND)
-        v = d_ref[m, u] * here
+        v = held[n][u] * here
         hi = v.astype(bf)
         lhi[m, q] = hi
         llo[m, q] = (v - hi.astype(f32)).astype(bf)
-        w = d_ref[m, u, :, pl.ds(col, half)] * here
+        w = held[n][u, :, pl.ds(col, half)] * here
         whi = w.astype(bf)
         phi[3 + m, q] = whi
         plo[m, q] = (w - whi.astype(f32)).astype(bf)
 
-    for m in range(rows):
+    for n in range(rows):
         for q in range(SPAN):
-            lay(m, q)
-        pump()
+            lay(n, q)
+            if q in (3, 6):
+                pump()
 
     def right(ref, k, d):
         lo, hi = max(0, -d), min(SPAN, SPAN - d)
@@ -230,14 +238,6 @@
         d = k - 3 - i
         hi, e0 = right(phi, k, d)
         add(acc, i, dot(lhi[i, d + BAND], hi) + dot(llo[i, d + BAND], hi), e0)
-
-    for i in range(rows):
-        for m in range(rows):
-            local_square(i, m)
-            pump()
-
-    while state["y"] < 18:
-        pump()
 
     def spread(side_up, get, n, m):
         k = (6 if side_up else 0) + m
@@ -254,63 +254,118 @@
                 prev = prev + get(n, q).astype(f32) * (lack > o).astype(f32)
             phi[k, q] = prev.astype(bf)
 
-    @pl.when(x == 0)
-    def _():
-        for n in range(3):
-            spread(True, lambda n, q: xin[n, q], n, 2 - n)
-
-    @pl.when(x == 1)
-    def _():
-        for n in range(3):
-            spread(False, lambda n, q: xin[n, q], n, n)
-
-    @pl.when(outer)
-    def _():
-        for k in range(15):
-            zcopy(k).wait_recv()
-
-    for is_outer, ref in ((True, zin), (False, yin)):
-        cond = outer if is_outer else jnp.logical_not(outer)
-
-        @pl.when(cond & (x == 0))
-        def _(ref=ref):
-            for n in range(3):
-                spread(False, lambda n, q: ref[n, q - n], n, 2 - n)
-
-        @pl.when(cond & (x == 1))
-        def _(ref=ref):
-            for n in range(3):
-                spread(True, lambda n, q: ref[n, q], n, n)
-
-    scopies = []
+    def by_side(step):
+        for side in (0, 1):
+            @pl.when(x == side)
+            def _(side=side):
+                step(side)
+
+    def x_row(n):
+        def step(side):
+            m = n if side else 2 - n
+            spread(side == 0, lambda n, q: xin[n, q], n, m)
+            if side:
+                for i in range(n + 1):
+                    far_square(i, n)
+            else:
+                for i in range(2 - n, rows):
+                    far_square(i, 8 - n)
+        by_side(step)
+
+    def w_row(n):
+        span = range(*((0, 6), (6, 11), (11, 15))[n])
+
+        @pl.when(outer)
+        def _():
+            for k in span:
+                zcopy(k).wait_recv()
+
+        def step(side):
+            m = n if side else 2 - n
+            for ref, cond in ((zin, outer), (yin, jnp.logical_not(outer))):
+                @pl.when(cond)
+                def _(ref=ref):
+                    if side:
+                        spread(True, lambda n, q: ref[n, q], n, n)
+                    else:
+                        spread(False, lambda n, q: ref[n, q - n], n, 2 - n)
+            if side:
+                for i in range(n, rows):
+                    far_square(i, 6 + n)
+            else:
+                for i in range(3 - n):
+                    far_square(i, 2 - n)
+        by_side(step)
+
+    def row_at(j):
+        return jnp.where(x == 1, j, 2 - j)
+
+    def swap(j):
+        i = row_at(j)
+        return pltpu.make_async_remote_copy(
+            src_ref=sl.at[layer, i], dst_ref=sl.at[layer, i], send_sem=ss.at[j], recv_sem=sr.at[j],
+            device_id=(1 - layer, b), device_id_type=MESH)
+
+    def swap_in(j):
+        i = row_at(j)
+        return pltpu.make_async_remote_copy(
+            src_ref=sl.at[1 - layer, i], dst_ref=sl.at[1 - layer, i], send_sem=ss.at[j], recv_sem=sr.at[j],
+            device_id=(1 - layer, b), device_id_type=MESH)
+
+    def share(j):
+        def step(side):
+            i = j if side else 2 - j
+            for q in range(SPAN):
+                here = (row_lack[i] != q - BAND).astype(f32)
+                sl[layer, i, q] = (acc[i, q] * here).astype(bf)
+        by_side(step)
+        swap(j).start()
+
+    def cube(j):
+        swap_in(j).wait_recv()
+
+        def step(side):
+            i = j if side else 2 - j
+            for k in range(i, i + SPAN):
+                d = k - 3 - i
+                a = jnp.concatenate([sl[0, i, d + BAND], sl[1, i, d + BAND]], axis=1)
+                hi, e0 = right(phi, k, d)
+                v = dot(a, hi)
+                if 3 <= k < 6:
+                    lo, _ = right(plo, k - 3, d)
+                    v = v + dot(a, lo)
+                add(cub, i, v, e0)
+            for q in range(SPAN):
+                cub[i, q] = 3.0 * acc[i, q] - 2.0 * cub[i, q]
+        by_side(step)
+
     for i in range(rows):
-        for k in list(range(i, 3)) + list(range(6, 7 + i)):
-            far_square(i, k)
-        for q in range(SPAN):
-            here = (row_lack[i] != q - BAND).astype(f32)
-            sl[layer, i, q] = (acc[i, q] * here).astype(bf)
-        cp = pltpu.make_async_remote_copy(
-            src_ref=sl.at[layer, i], dst_ref=sl.at[layer, i], send_sem=ss.at[i], recv_sem=sr.at[i],
-            device_id=(1 - layer, b), device_id_type=MESH)
-        cp.start()
-        scopies.append(cp)
-
-    for i in range(rows):
-        scopies[i].wait_send()
-        pltpu.make_async_remote_copy(
-            src_ref=sl.at[1 - layer, i], dst_ref=sl.at[1 - layer, i], send_sem=ss.at[i], recv_sem=sr.at[i],
-            device_id=(1 - layer, b), device_id_type=MESH).wait_recv()
-        for k in range(i, i + SPAN):
-            d = k - 3 - i
-            a = jnp.concatenate([sl[0, i, d + BAND], sl[1, i, d + BAND]], axis=1)
-            hi, e0 = right(phi, k, d)
-            v = dot(a, hi)
-            if 3 <= k < 6:
-                lo, _ = right(plo, k - 3, d)
-                v = v + dot(a, lo)
-            add(cub, i, v, e0)
-        for q in range(SPAN):
-            cub[i, q] = 3.0 * acc[i, q] - 2.0 * cub[i, q]
+        for m in range(rows):
+            local_square(i, m)
+            if state["y"] < 14:
+                pump()
+    while state["y"] < 14:
+        pump()
+    x_row(0)
+    pump()
+    w_row(0)
+    pump()
+    pump()
+    x_row(1)
+    pump()
+    w_row(1)
+    while state["y"] < 18:
+        pump()
+    x_row(2)
+    share(0)
+    share(1)
+    cube(0)
+    w_row(2)
+    share(2)
+    cube(1)
+    cube(2)
+    for j in range(rows):
+        swap(j).wait_send()
 
     for cp in sends:
         cp.wait_send()
@@ -344,16 +399,19 @@
     rows, slots, order, _ = density.shape
     half = order // 2
     dense = pltpu.VMEM((rows, SPAN, order, half), jnp.float32)
-    vmem, smem, anyspace = (pl.BlockSpec(memory_space=m) for m in (pltpu.VMEM, pltpu.SMEM, pl.ANY))
+    vmem, smem, hbm = (pl.BlockSpec(memory_space=m) for m in (pltpu.VMEM, pltpu.SMEM, pltpu.HBM))
     bf, f32 = jnp.bfloat16, jnp.float32
     dma = pltpu.SemaphoreType.DMA
     block = (order, half)
     sq, pu = pl.pallas_call(
         step_kernel,
         out_shape=[dense, dense],
-        in_specs=[smem, vmem],
+        in_specs=[smem, hbm],
         out_specs=[vmem, vmem],
         scratch_shapes=[
+            pltpu.VMEM((slots, order, order), f32),
+            pltpu.VMEM((slots, order, order), f32),
+            pltpu.VMEM((slots, order, order), f32),
             pltpu.VMEM((3, 6) + block, bf),
             pltpu.VMEM((3, 6) + block, bf),
             pltpu.VMEM((3, 6) + block, bf),
@@ -364,7 +422,7 @@
             pltpu.VMEM((rows, SPAN) + block, bf),
             pltpu.VMEM((2, rows, SPAN) + block, bf),
             dma((18,)), dma((18,)), dma((15,)), dma((15,)), dma((15,)), dma((15,)),
-            dma((3,)), dma((3,)),
+            dma((3,)), dma((3,)), dma((3,)),
         ],
         compiler_params=pltpu.CompilerParams(
             collective_id=0, has_side_effects=True, vmem_limit_bytes=40 * 1024 * 1024),
@@ -375,8 +433,9 @@
         place_kernel,
         out_shape=[out, out],
         in_specs=[smem, vmem, vmem],
-        out_specs=[anyspace, anyspace],
+        out_specs=[hbm, hbm],
         scratch_shapes=[dma((2, rows, slots))],
+        compiler_params=pltpu.CompilerParams(vmem_limit_bytes=4 * 1024 * 1024),
     )(pattern, sq, pu)
 
 

time: 64.7 us -> 59.8 us (0.924)
  local copies, waits for them, and re-layouts: 6.23 us -> 3.11 us
  Pallas kernels: 57.5 us -> 55.7 us
    unnamed x9 -> x3, local copies, waits for them, and re-layouts: 6.23 us -> 3.11 us
    pallas_call x1, Pallas kernels: 5.09 us -> 3.41 us  [fused(): pl.pallas_call(place_kernel, out_shape=[out, out], in_specs=[smem, vmem,...]
where the time goes in v3:
time: 59.8 us; the launch traced here: 59.6 us
  Pallas kernels  55.7 us (93%)
  local copies, waits for them, and re-layouts  3.11 us (5%)
  between operations  0.8 us (1%)
    pallas_call x1, Pallas kernels, fused(): pl.pallas_call(step_kernel, out_shape=[dense, dense], in_specs=[smem, hbm...  52.3 us
    pallas_call x1, Pallas kernels, fused(): pl.pallas_call(place_kernel, out_shape=[out, out], in_specs=[smem, vmem,...  3.41 us
    unnamed x3, local copies, waits for them, and re-layouts  3.11 us

profile of v3, /device:TPU:0, one launch (start us, length us, event | category | flops | bytes accessed | tf_op | source)
XLA Modules:
  0.0 59.6 jit_solution(8453160717604542485)
XLA Ops:
  0.6 0.8 %copy.5.pattern_ref = s32[48,6]{1,0:T(8,128)S(1)} copy(s32[48,6]{0,1:T(8,128)} %param.3) | data formatting | bytes 2304 | tf_op args[1]
  1.4 0.0 copy-start
  1.4 2.3 %copy-done = f32[3,6,256,256]{3,2,1,0:T(8,128)S(1)} copy-done((f32[3,6,256,256]{3,2,1,0:T(8,128)S(1)}, f32[3,6,256,256]{3,2,1,0:T(8,128)}, u32[]{:S(2)}) %copy-start) | copy-done | bytes 4718616
  3.7 52.3 %shard_map.41 = (f32[3,7,256,128]{3,2,1,0:T(8,128)S(1)}, f32[3,7,256,128]{3,2,1,0:T(8,128)S(1)}) custom-call(s32[48,6]{1,0:T(8,128)S(1)} %copy.5.pattern_ref, f32[3,6,256,256]{3,2,1,0:T(8,128)S(1)} %copy-done), custom_call_target="tpu_custom_call" | custom-call | flops 10000000000 | bytes 10000000 | tf_op jit(solution)/shard_map/pallas_call | solution.py:406
  56.0 3.4 %shard_map.42 = (f32[3,6,256,128]{3,2,1,0:T(8,128)}, f32[3,6,256,128]{3,2,1,0:T(8,128)}) custom-call(s32[48,6]{1,0:T(8,128)S(1)} %copy.5.pattern_ref, f32[3,7,256,128]{3,2,1,0:T(8,128)S(1)} %get-tuple-element.4.sq, f32[3,7,256,128]{3,2,1,0:T(8,128)S(1)} %get-tuple-element.5.pu), custom_call_target="tpu_custom_call" | custom-call | tf_op jit(solution)/shard_map/pallas_call | solution.py:432
Async XLA Ops:
  1.4 2.3 %copy-start = (f32[3,6,256,256]{3,2,1,0:T(8,128)S(1)}, f32[3,6,256,256]{3,2,1,0:T(8,128)}, u32[]{:S(2)}) copy-start(f32[3,6,256,256]{3,2,1,0:T(8,128)} %d_hbm.1) | copy-start | bytes 14155780
